TPU v7x, 256 devices: a whole 4x4x8 slice. The times are simulated.
256 devices in a mesh: attn: 64 (over x, z_hi, y, core), ffn: 4 (over z_lo).
Axes of the slice: x: 4, y: 4, z: 8 (z_hi: 2, z_lo: 4; z = z_hi * 4 + z_lo), core: 2. Of those that a mesh axis runs over, the one named last changes fastest.
Arguments:
- queries: bfloat16 [512, 8192], P('attn', 'ffn'), may hold values from -132 to 132
- cache_keys: bfloat16 [512, 512, 512], P('attn', None, 'ffn'), may hold values from -6 to 6
- value_cache: bfloat16 [512, 512, 512], P('attn', None, 'ffn'), may hold values from -6 to 6
- new_keys: bfloat16 [512, 512], P('attn', 'ffn'), may hold values from -6 to 6
- token_values: bfloat16 [512, 512], P('attn', 'ffn'), may hold values from -6 to 6
- lengths: int32 [512], P('attn'), may hold values from 1 to 512, 87381 in all
- norm_gain: float32 [8192], P('ffn'), may hold values from 0.1 to 1.9
- w_gate: bfloat16 [8192, 40960], P('ffn', 'attn'), may hold values from -0.0625 to 0.0625
- w_up: bfloat16 [8192, 40960], P('ffn', 'attn'), may hold values from -0.0625 to 0.0625
- w_down: bfloat16 [40960, 8192], P('attn', 'ffn'), may hold values from -0.03125 to 0.03125
Outputs:
- attn_out: bfloat16 [512, 8192], P('attn', 'ffn')
- ffn_out: bfloat16 [512, 8192], P('attn', 'ffn')
All inputs are finite; a program needn't handle non-finite values. No bound on the sum of `lengths` on one device may be relied on, other than what follows from the above.
Results may differ from a plain program's by a relative error of at most 0.013.
Values may be sent and summed in bfloat16 or wider, within the bound.
A program may use at most 128 MiB of HBM per device.

v0:
```python
import jax
import jax.numpy as jnp
from jax import lax
from jax.sharding import PartitionSpec as P

D = 8192


def attend_block(queries, cache_keys, value_cache, new_keys, token_values, lengths):
    head_size = new_keys.shape[1]
    requests = queries.shape[0]
    group_width = queries.shape[1] // head_size
    capacity = cache_keys.shape[1]
    scaling = 1.0 / head_size**0.5
    heads_query = queries.reshape(requests, group_width, head_size)
    scores = (
        jnp.einsum("rgd,rjd->rgj", heads_query, cache_keys, preferred_element_type=jnp.float32)
        * scaling
    )
    own_score = (
        jnp.einsum("rgd,rd->rg", heads_query, new_keys, preferred_element_type=jnp.float32)
        * scaling
    )
    live_mask = jnp.arange(capacity, dtype=jnp.int32)[None, :] < lengths[:, None]
    scores = jnp.where(live_mask[:, None, :], scores, -1e30)
    largest = jnp.maximum(jnp.max(scores, axis=-1), own_score)
    weights = jnp.where(live_mask[:, None, :], jnp.exp(scores - largest[..., None]), 0.0)
    own_weight = jnp.exp(own_score - largest)
    denominator = jnp.sum(weights, axis=-1) + own_weight
    probs = (weights / denominator[..., None]).astype(jnp.bfloat16)
    own_prob = (own_weight / denominator).astype(jnp.bfloat16)
    attended = jnp.einsum("rgj,rjd->rgd", probs, value_cache, preferred_element_type=jnp.float32)
    attended = (
        attended
        + own_prob.astype(jnp.float32)[..., None] * token_values.astype(jnp.float32)[:, None, :]
    )
    return attended.reshape(requests, group_width * head_size).astype(jnp.bfloat16)


def local(
    queries,
    cache_keys,
    value_cache,
    new_keys,
    token_values,
    lengths,
    norm_gain,
    w_gate,
    w_up,
    w_down,
):
    attn_out = attend_block(queries, cache_keys, value_cache, new_keys, token_values, lengths)
    features = attn_out.astype(jnp.float32)
    square_sum = lax.psum(jnp.sum(features * features, axis=-1), "ffn")
    mean_square = square_sum / D
    normed = (features * lax.rsqrt(mean_square + 1e-05)[:, None] * norm_gain[None, :]).astype(
        jnp.bfloat16
    )
    block_rows = lax.all_gather(normed, "attn", axis=0, tiled=True)
    gate_part = jnp.dot(block_rows, w_gate, preferred_element_type=jnp.float32)
    up_part = jnp.dot(block_rows, w_up, preferred_element_type=jnp.float32)
    partials = jnp.stack([gate_part, up_part])
    whole_sums = lax.psum(partials, "ffn")
    all_units = (jax.nn.silu(whole_sums[0]) * whole_sums[1]).astype(jnp.bfloat16)
    ffn_out = lax.psum_scatter(
        jnp.dot(all_units, w_down, preferred_element_type=jnp.float32),
        "attn",
        scatter_dimension=0,
        tiled=True,
    ).astype(jnp.bfloat16)
    return (attn_out, ffn_out)


def solution(mesh):
    in_specs = (
        P("attn", "ffn"),
        P("attn", None, "ffn"),
        P("attn", None, "ffn"),
        P("attn", "ffn"),
        P("attn", "ffn"),
        P("attn"),
        P("ffn"),
        P("ffn", "attn"),
        P("ffn", "attn"),
        P("attn", "ffn"),
    )
    out_specs = (P("attn", "ffn"), P("attn", "ffn"))
    return jax.shard_map(local, mesh=mesh, in_specs=in_specs, out_specs=out_specs, check_vma=False)
```

profile of v0, /device:TPU:32, one launch (start us, length us, event | category | flops | bytes accessed | tf_op | source)
XLA Modules:
  0.0 657.6 jit_solution(7649183414724110605)
XLA Ops:
  7.2 0.0 copy-start
  7.2 0.0 copy-start.1
  7.2 0.0 all-gather.2.cloned.1.call-start
  7.2 0.9 iota_compare_fusion
  8.1 0.7 convert_element_type.37
  8.8 0.9 fusion.12
  9.7 1.7 fusion.20
  11.4 0.2 fusion.7
  11.6 1.6 multiply_reduce_fusion
  13.3 10.1 %psum.14 = f32[8]{0:T(128)S(1)} all-reduce(f32[8]{0:T(128)S(1)} %get-tuple-element.8), channel_id=1, replica_groups=mesh['attn'=64,'ffn'=4] {'ffn'}, use_global_device_ids=true, to_apply=%region_3.4 | all-reduce | flops 8 | bytes 64 | tf_op jit(solution)/shard_map/psum | solution.py:54
  23.4 0.0 copy-done.1
  23.4 0.7 multiply_convert_fusion
  24.1 0.0 all-gather.2.cloned.1.call-update
  24.1 0.0 all-reduce.2.cloned.1.call-start
  24.2 84.1 %all-gather.2.cloned.1.call-done = bf16[512,2048]{1,0:T(8,128)(2,1)} async-done(((bf16[8,2048]{1,0:T(8,128)(2,1)}), bf16[512,2048]{1,0:T(8,128)(2,1)}) %all-gather.2.cloned.1.call-update) | async-done | bytes 2097168 | tf_op jit(solution)/shard_map/all_gather | solution.py:59
  108.3 0.0 copy-start.2
  108.3 0.0 copy-start.3
  108.3 4.3 convolution_bitcast_fusion
  112.6 0.0 copy-done.2
  112.6 0.0 copy-done.3
  112.6 1.8 convolution_bitcast_fusion.1
  114.4 1.7 pad_maximum_fusion
  116.1 0.0 all-reduce.2.cloned.1.call-update
  116.1 0.0 reduce-scatter.2.cloned.1.call-start
  116.2 109.6 %all-reduce.2.cloned.1.call-done = f32[2,512,640]{2,1,0:T(8,128)} async-done(((f32[2,512,640]{2,1,0:T(8,128)}), f32[2,512,640]{2,1,0:T(8,128)}) %all-reduce.2.cloned.1.call-update) | async-done | bytes 2621456 | tf_op jit(solution)/shard_map/psum | solution.py:63
  225.7 0.0 copy-done
  225.7 5.5 fusion.4
  231.2 0.0 reduce-scatter.2.cloned.1.call-update
  231.2 418.4 %reduce-scatter.2.cloned.1.call-done = f32[8,2048]{1,0:T(8,128)} async-done(((f32[512,2048]{1,0:T(8,128)}), f32[8,2048]{1,0:T(8,128)}) %reduce-scatter.2.cloned.1.call-update) | async-done | bytes 65552 | tf_op jit(solution)/shard_map/reduce_scatter | solution.py:65
  649.6 1.5 convert_element_type.44
  (3 shorter events, 0.0 us)
Async XLA Ops:
  7.2 218.6 %copy-start = (bf16[640,2048]{1,0:T(8,128)(2,1)S(1)}, bf16[640,2048]{1,0:T(8,128)(2,1)}, u32[]{:S(2)}) copy-start(bf16[640,2048]{1,0:T(8,128)(2,1)} %param.19) | copy-start | bytes 7864324
  7.2 16.2 %copy-start.1 = (f32[2048]{0:T(1024)S(1)}, f32[2048]{0:T(1024)}, u32[]{:S(2)}) copy-start(f32[2048]{0:T(1024)} %param.16) | copy-start | bytes 24580
  7.2 101.1 %all-gather.2.cloned.1.call-start = ((), (), s32[]{:S(2)}) async-start(), calls=%async_computation.1 | async-start | bytes 2129920 | tf_op jit(solution)/shard_map/all_gather | solution.py:59
  24.1 201.6 %all-reduce.2.cloned.1.call-start = ((), (), s32[]{:S(2)}) async-start(), calls=%async_computation.2 | async-start | bytes 5242880 | tf_op jit(solution)/shard_map/psum | solution.py:63
  108.3 4.3 copy-start.2
  108.3 4.3 copy-start.3
  116.1 533.5 %reduce-scatter.2.cloned.1.call-start = ((), (), s32[]{:S(2)}) async-start(), calls=%async_computation.3 | async-start | bytes 4259840 | tf_op jit(solution)/shard_map/reduce_scatter | solution.py:65
Sparse Core Ops, SparseCore 0:
  24.3 83.9 all-gather.1
  116.2 109.4 all-reduce.1
  231.3 418.2 reduce-scatter.1
where the time goes:
time: 658 us
  waiting for transfers between devices  612 us (93%)
  matrix products  15.8 us (2%)
  between operations  13.8 us (2%)
  blocking collectives  10.1 us (2%)
    reduce_scatter x1, waiting for transfers between devices, local(): lax.psum_scatter(jnp.dot(all_units, w_down, preferred_element_type=jnp.fl...  418 us
    psum x1, waiting for transfers between devices, local(): whole_sums = lax.psum(partials, 'ffn')  110 us
    all_gather x1, waiting for transfers between devices, local(): block_rows = lax.all_gather(normed, 'attn', axis=0, tiled=True)  84.1 us
  transfers between devices with their start and end apart: 3, of which 3 were waited for; matrix products, arithmetic and copies ran while one was open for 0% of the time, Pallas kernels for 0%

commit v1 on v0

v1 whole, which is shorter than its diff:
```python
import functools

import jax
import jax.numpy as jnp
from jax import lax
from jax.experimental import pallas as pl
from jax.experimental.pallas import tpu as pltpu
from jax.sharding import PartitionSpec as P

MESH = pl.DeviceIdType.MESH
F32, BF16 = jnp.float32, jnp.bfloat16
D = 8192
CHUNKS = 8
ROWS = 64
PART = 32
UNITS = 640
LAST = 3


def chunk_of(j, x, zh):
    i = j // 2
    dx = i + (i // 2) * (5 - 2 * i)
    flip = (j + (j + 6) // 8) % 2
    return dx, flip, ((x + dx) % 4) * 2 + (zh + flip) % 2


def kernel(
    q_ref, nk_ref, tv_ref, len_ref, gain_ref, k_hbm, v_hbm, wg_hbm, wu_hbm, wd_hbm,
    attn_ref, out_ref,
    kbuf, vbuf, wgu, wd, qs, os, ssr, xblk, xall, part, sbuf, rbuf, hbuf, cs, cr, acc, xcs, xcr, zcs, zcr,
    load_sem, ss_send, ss_recv, z_send, z_recv, y_send, y_recv, x_send, x_recv, f_send, f_recv,
    r_send, r_recv, h_send, h_recv, c_send, c_recv, xc_send, xc_recv, zc_send, zc_recv,
):
    a = lax.axis_index("attn")
    zl = lax.axis_index("ffn")
    c = a % 2
    y = (a // 2) % 4
    zh = (a // 8) % 2
    x = a // 16
    slot = y * 2 + c

    def at(x_, zh_, slot_, zl_=None):
        return {"attn": (x_ * 2 + zh_) * 8 + slot_, "ffn": zl if zl_ is None else zl_}

    sibling = at(x, zh, y * 2 + (1 - c))
    partner = at(x, 1 - zh, slot)

    def remote(src, dst, send, recv, device):
        return pltpu.make_async_remote_copy(
            src_ref=src, dst_ref=dst, send_sem=send, recv_sem=recv, device_id=device, device_id_type=MESH
        )

    loads = [
        pltpu.make_async_copy(k_hbm, kbuf, load_sem.at[0]),
        pltpu.make_async_copy(v_hbm, vbuf, load_sem.at[1]),
        pltpu.make_async_copy(wg_hbm, wgu.at[:, pl.ds(0, UNITS)], load_sem.at[2]),
        pltpu.make_async_copy(wu_hbm, wgu.at[:, pl.ds(UNITS, UNITS)], load_sem.at[3]),
        pltpu.make_async_copy(wd_hbm, wd, load_sem.at[4]),
    ]
    for load in loads:
        load.start()

    barrier = pltpu.get_barrier_semaphore()
    peers = [at(x, zh, (slot + d) % 8) for d in range(1, 8)]
    peers += [at((x + d) % 4, zh, slot) for d in range(1, 4)]
    peers += [at(x, zh, slot, (zl + d) % 4) for d in range(1, 4)]
    peers += [partner]
    for peer in peers:
        pl.semaphore_signal(barrier, inc=1, device_id=peer, device_id_type=MESH)

    qf = q_ref[...].astype(F32)
    for g in range(16):
        qs[pl.ds(g * 8, 8), :] = qf[:, g * 128 : (g + 1) * 128]
    nk = nk_ref[...].astype(F32)
    tv = tv_ref[...].astype(F32)
    loads[0].wait()
    loads[1].wait()
    scaling = 1.0 / 128**0.5
    position = lax.broadcasted_iota(jnp.int32, (16, 512), 1)
    for r in range(8):
        q = qs[pl.ds(r, 16, stride=8), :]
        scores = lax.dot_general(
            q.astype(BF16), kbuf[r], (((1,), (1,)), ((), ())), preferred_element_type=F32
        ) * scaling
        own = jnp.sum(q * nk[r : r + 1, :], axis=1, keepdims=True) * scaling
        live = position < len_ref[r]
        scores = jnp.where(live, scores, -1e30)
        largest = jnp.maximum(jnp.max(scores, axis=1, keepdims=True), own)
        weights = jnp.where(live, jnp.exp(scores - largest), 0.0)
        own_weight = jnp.exp(own - largest)
        total = jnp.sum(weights, axis=1, keepdims=True) + own_weight
        probs = (weights / total).astype(BF16)
        own_prob = (own_weight / total).astype(BF16).astype(F32)
        out = jnp.dot(probs, vbuf[r], preferred_element_type=F32)
        os[pl.ds(r, 16, stride=8), :] = out + own_prob * tv[r : r + 1, :]
    attn = jnp.concatenate([os[pl.ds(g * 8, 8), :] for g in range(16)], axis=1).astype(BF16)
    attn_ref[...] = attn
    feats = attn.astype(F32)
    ssr[zl] = jnp.broadcast_to(jnp.sum(feats * feats, axis=1, keepdims=True), (8, 128))

    pl.semaphore_wait(barrier, len(peers))

    def ss_copy(d):
        return remote(ssr.at[zl], ssr.at[zl], ss_send.at[d], ss_recv.at[zl], at(x, zh, slot, (zl + d) % 4))

    def ss_from(d):
        s = (zl + d) % 4
        return remote(ssr.at[s], ssr.at[s], ss_send.at[d], ss_recv.at[s], at(x, zh, slot, s))

    for d in range(1, 4):
        ss_copy(d).start()
    for d in range(1, 4):
        ss_from(d).wait_recv()
    squares = ssr[0] + ssr[1] + ssr[2] + ssr[3]
    scale = lax.rsqrt(squares[:, :1] / D + 1e-05)
    normed = feats * scale * gain_ref[...]
    xblk[0, slot] = jnp.concatenate([normed[:, :1024], normed[:, 1024:]], axis=0).astype(BF16)

    z_copy = remote(xblk.at[0, slot], xblk.at[1, slot], z_send, z_recv, partner)
    z_copy.start()

    def y_copy(w, d):
        return remote(
            xblk.at[w, slot], xblk.at[w, slot], y_send.at[w, d], y_recv.at[w, slot], at(x, zh, (slot + d) % 8)
        )

    def y_from(w, d):
        s = (slot + d) % 8
        return remote(xblk.at[w, s], xblk.at[w, s], y_send.at[w, d], y_recv.at[w, s], at(x, zh, s))

    def own_chunk(w):
        return x * 2 + (zh + w) % 2

    def x_copy(w, d):
        n = own_chunk(w)
        return remote(
            xall.at[n, c], xall.at[n, c], x_send.at[w, d], x_recv.at[n], at((x + d) % 4, zh, slot)
        )

    def assemble(w):
        n = own_chunk(w)
        for d in range(1, 8):
            y_from(w, d).wait_recv()
        for b in range(4):
            first = xblk[w, 2 * b].astype(F32)
            second = xblk[w, 2 * b + 1].astype(F32)
            for h in range(2):
                pair = [first[8 * h : 8 * h + 8], second[8 * h : 8 * h + 8]]
                xall[n, h, pl.ds(16 * b, 16), :] = jnp.concatenate(pair, axis=0).astype(BF16)
        for d in (1, 3, 2):
            x_copy(w, d).start()

    for d in range(1, 8):
        y_copy(0, d).start()
    z_copy.wait_recv()
    for d in range(1, 8):
        y_copy(1, d).start()
    assemble(0)
    for load in loads[2:]:
        load.wait()

    positions = [zl, LAST - zl]
    nexts = [at(x, zh, slot, (zl + 1) % 4), at(x, zh, slot, (zl + 3) % 4)]
    backs = [nexts[1], nexts[0]]

    def r_copy(dr, j):
        return remote(sbuf.at[dr, j], rbuf.at[dr, j], r_send.at[dr, j], r_recv.at[dr, j], nexts[dr])

    def h_copy(dr, j):
        piece = hbuf.at[j, pl.ds(dr * PART, PART)]
        return remote(piece, piece, h_send.at[dr, j], h_recv.at[dr, j], backs[dr])

    def forward(j):
        n = chunk_of(j, x, zh)[2]
        return remote(xall.at[n, c], xall.at[n, c], f_send.at[j], f_recv.at[j], sibling)

    def forwarded(j):
        n = chunk_of(j, x, zh)[2]
        return remote(xall.at[n, 1 - c], xall.at[n, 1 - c], f_send.at[j], f_recv.at[j], sibling)

    def x_from(j):
        dx, _, n = chunk_of(j, x, zh)
        return remote(xall.at[n, c], xall.at[n, c], f_send.at[j], x_recv.at[n], at((x + dx) % 4, zh, slot))

    def c_copy(j, d):
        s = (slot + d) % 8
        return remote(cs.at[j, s], cr.at[j, slot], c_send.at[j, d], c_recv.at[j, slot], at(x, zh, s))

    def c_from(j, d):
        s = (slot + d) % 8
        return remote(cs.at[j, s], cr.at[j, s], c_send.at[j, d], c_recv.at[j, s], at(x, zh, s))

    def xc_copy(flip, dx):
        k = dx - 1
        return remote(
            xcs.at[flip, k], xcr.at[flip, k], xc_send.at[flip, k], xc_recv.at[flip, k], at((x + dx) % 4, zh, slot)
        )

    def body(i, carry):
        for dr in range(2):
            p = positions[dr]
            j = i - p

            @pl.when((p > 0) & (j >= 0) & (j < CHUNKS))
            def _():
                r_copy(dr, j).wait_recv()
                sums = part[j, pl.ds(dr * PART, PART), :] + rbuf[dr, j].astype(F32)

                @pl.when(p < LAST)
                def _():
                    sbuf[dr, j] = sums.astype(BF16)
                    r_copy(dr, j).start()

                @pl.when(p == LAST)
                def _():
                    gate, up = sums[:, :UNITS], sums[:, UNITS:]
                    hidden = gate / (1.0 + jnp.exp(-gate)) * up
                    hbuf[j, pl.ds(dr * PART, PART), :] = hidden.astype(BF16)
                    h_copy(dr, j).start()

        for dr in range(2):
            p = positions[dr]
            j = i - (2 * LAST - p)

            @pl.when((p < LAST) & (j >= 0) & (j < CHUNKS))
            def _():
                h_copy(dr, j).wait_recv()

                @pl.when(p > 0)
                def _():
                    h_copy(dr, j).start()

        @pl.when(i < CHUNKS)
        def _():
            @pl.when(i >= 2)
            def _():
                forwarded(i).wait_recv()

            n = chunk_of(i, x, zh)[2]
            for t in range(5):
                cols = pl.ds(t * 256, 256)
                part[i, :, cols] = jnp.dot(
                    xall[n, 0], wgu[pl.ds(0, 1024), cols], preferred_element_type=F32
                ) + jnp.dot(xall[n, 1], wgu[pl.ds(1024, 1024), cols], preferred_element_type=F32)
            for dr in range(2):

                @pl.when(positions[dr] == 0)
                def _():
                    sbuf[dr, i] = part[i, pl.ds(dr * PART, PART), :].astype(BF16)
                    r_copy(dr, i).start()

        @pl.when(i == 0)
        def _():
            assemble(1)

        @pl.when((i >= 1) & (i < CHUNKS - 1))
        def _():
            x_from(i + 1).wait_recv()
            forward(i + 1).start()

        j = i - 2 * LAST

        @pl.when((j >= 0) & (j < CHUNKS))
        def _():
            hidden = hbuf[j]
            for t in range(4):
                left = jnp.dot(hidden, wd[:, pl.ds(t * 256, 256)], preferred_element_type=F32)
                right = jnp.dot(hidden, wd[:, pl.ds(1024 + t * 256, 256)], preferred_element_type=F32)
                for b in range(8):
                    block = jnp.concatenate([left[b * 8 : b * 8 + 8], right[b * 8 : b * 8 + 8]], axis=0)
                    cs[j, b, :, pl.ds(t * 256, 256)] = block.astype(BF16)
            for d in range(1, 8):
                c_copy(j, d).start()
            cr[j, slot] = cs[j, slot]

        m = i - 2 * LAST - 1

        @pl.when(m >= 0)
        def _():
            for d in range(1, 8):
                c_from(m, d).wait_recv()
            total = cr[m, 0].astype(F32)
            for b in range(1, 8):
                total = total + cr[m, b].astype(F32)
            dx, flip, _ = chunk_of(m, x, zh)

            @pl.when(m < 2)
            def _():
                acc[flip] = total

            @pl.when(m >= 2)
            def _():
                xcs[flip, dx - 1] = total.astype(BF16)
                xc_copy(flip, dx).start()

        return carry

    lax.fori_loop(0, CHUNKS + 2 * LAST + 1, body, 0)

    sums = []
    zc_copy = remote(zcs, zcr, zc_send, zc_recv, partner)
    for flip in (1, 0):
        for dx in range(1, 4):
            xc_copy(flip, dx).wait_recv()
        total = acc[flip]
        for dx in range(1, 4):
            total = total + xcr[flip, dx - 1].astype(F32)
        if flip == 1:
            zcs[...] = total.astype(BF16)
            zc_copy.start()
    zc_copy.wait_recv()
    total = total + zcr[...].astype(F32)
    out_ref[...] = jnp.concatenate([total[:8], total[8:]], axis=1).astype(BF16)

    zc_copy.wait_send()
    z_copy.wait_send()
    for d in range(1, 4):
        ss_copy(d).wait_send()
        for w in range(2):
            x_copy(w, d).wait_send()
            xc_copy(w, d).wait_send()
    for d in range(1, 8):
        for w in range(2):
            y_copy(w, d).wait_send()

    def drain(j, carry):
        @pl.when(j >= 2)
        def _():
            forward(j).wait_send()

        for d in range(1, 8):
            c_copy(j, d).wait_send()
        for dr in range(2):

            @pl.when(positions[dr] < LAST)
            def _():
                r_copy(dr, j).wait_send()

            @pl.when(positions[dr] > 0)
            def _():
                h_copy(dr, j).wait_send()

        return carry

    lax.fori_loop(0, CHUNKS, drain, 0)


def local(queries, cache_keys, value_cache, new_keys, token_values, lengths, norm_gain, w_gate, w_up, w_down):
    vmem = pl.BlockSpec(memory_space=pltpu.VMEM)
    hbm = pl.BlockSpec(memory_space=pl.ANY)
    dma = pltpu.SemaphoreType.DMA
    return pl.pallas_call(
        kernel,
        out_shape=(jax.ShapeDtypeStruct((8, 2048), BF16), jax.ShapeDtypeStruct((8, 2048), BF16)),
        in_specs=[vmem, vmem, vmem, pl.BlockSpec(memory_space=pltpu.SMEM), vmem] + [hbm] * 5,
        out_specs=(vmem, vmem),
        scratch_shapes=[
            pltpu.VMEM((8, 512, 128), BF16),
            pltpu.VMEM((8, 512, 128), BF16),
            pltpu.VMEM((2048, 2 * UNITS), BF16),
            pltpu.VMEM((UNITS, 2048), BF16),
            pltpu.VMEM((128, 128), F32),
            pltpu.VMEM((128, 128), F32),
            pltpu.VMEM((4, 8, 128), F32),
            pltpu.VMEM((2, 8, 16, 1024), BF16),
            pltpu.VMEM((CHUNKS, 2, ROWS, 1024), BF16),
            pltpu.VMEM((CHUNKS, ROWS, 2 * UNITS), F32),
            pltpu.VMEM((2, CHUNKS, PART, 2 * UNITS), BF16),
            pltpu.VMEM((2, CHUNKS, PART, 2 * UNITS), BF16),
            pltpu.VMEM((CHUNKS, ROWS, UNITS), BF16),
            pltpu.VMEM((CHUNKS, 8, 16, 1024), BF16),
            pltpu.VMEM((CHUNKS, 8, 16, 1024), BF16),
            pltpu.VMEM((2, 16, 1024), F32),
            pltpu.VMEM((2, 3, 16, 1024), BF16),
            pltpu.VMEM((2, 3, 16, 1024), BF16),
            pltpu.VMEM((16, 1024), BF16),
            pltpu.VMEM((16, 1024), BF16),
            dma((5,)),
            dma((4,)), dma((4,)),
            dma, dma,
            dma((2, 8)), dma((2, 8)),
            dma((2, 4)), dma((CHUNKS,)),
            dma((CHUNKS,)), dma((CHUNKS,)),
            dma((2, CHUNKS)), dma((2, CHUNKS)),
            dma((2, CHUNKS)), dma((2, CHUNKS)),
            dma((CHUNKS, 8)), dma((CHUNKS, 8)),
            dma((2, 3)), dma((2, 3)),
            dma, dma,
        ],
        compiler_params=pltpu.CompilerParams(
            collective_id=0, has_side_effects=True, vmem_limit_bytes=50 * 1024 * 1024
        ),
    )(queries, new_keys, token_values, lengths, norm_gain.reshape(1, 2048), cache_keys, value_cache, w_gate, w_up, w_down)


def solution(mesh):
    in_specs = (
        P("attn", "ffn"),
        P("attn", None, "ffn"),
        P("attn", None, "ffn"),
        P("attn", "ffn"),
        P("attn", "ffn"),
        P("attn"),
        P("ffn"),
        P("ffn", "attn"),
        P("ffn", "attn"),
        P("attn", "ffn"),
    )
    out_specs = (P("attn", "ffn"), P("attn", "ffn"))
    return jax.shard_map(local, mesh=mesh, in_specs=in_specs, out_specs=out_specs, check_vma=False)
```

time: 658 us -> 96.6 us (0.15)
  the two profiles are of different devices: /device:TPU:32 before, /device:TPU:2 now
where the time goes in v1:
time: 96.6 us; the launch traced here: 95.8 us
  Pallas kernels  88 us (91%)
  local copies, waits for them, and re-layouts  7.14 us (7%)
    pallas_call x1, Pallas kernels, local(): pl.pallas_call(kernel, out_shape=(jax.ShapeDtypeStruct((8, 2048), BF16),...  88 us
    unnamed x16, local copies, waits for them, and re-layouts  7.14 us

profile of v1, /device:TPU:2, one launch (start us, length us, event | category | flops | bytes accessed | tf_op | source)
XLA Modules:
  0.0 95.8 jit_solution(1945075515781364659)
XLA Ops:
  0.6 0.0 copy-start
  0.6 1.2 %copy-done = bf16[8,512,128]{2,1,0:T(8,128)(2,1)S(1)} copy-done((bf16[8,512,128]{2,1,0:T(8,128)(2,1)S(1)}, bf16[8,512,128]{2,1,0:T(8,128)(2,1)}, u32[]{:S(2)}) %copy-start) | copy-done | bytes 1048600
  1.9 0.0 copy-start.1
  1.9 1.2 %copy-done.1 = bf16[8,512,128]{2,1,0:T(8,128)(2,1)S(1)} copy-done((bf16[8,512,128]{2,1,0:T(8,128)(2,1)S(1)}, bf16[8,512,128]{2,1,0:T(8,128)(2,1)}, u32[]{:S(2)}) %copy-start.1) | copy-done | bytes 1048600
  3.1 0.0 copy-start.2
  3.1 0.8 copy-done.2
  3.8 0.0 copy-start.3
  3.8 0.7 copy-done.3
  4.5 0.0 copy-start.4
  4.5 0.7 copy-done.4
  5.2 0.0 copy-start.5
  5.2 0.7 copy-done.5
  5.9 0.0 copy-start.6
  5.9 0.7 copy-done.6
  6.6 88.0 %shard_map.113 = (bf16[8,2048]{1,0:T(8,128)(2,1)S(1)}, bf16[8,2048]{1,0:T(8,128)(2,1)S(1)}) custom-call(bf16[8,2048]{1,0:T(8,128)(2,1)S(1)} %copy-done.2, bf16[8,128]{1,0:T(8,128)(2,1)S(1)} %copy-done.4, bf16[8,128]{1,0:T(8,128)(2,1)S(1)} %copy-done.5, s32[8]{0:T(128)S(1)} %copy-done.6, f32[1,2048]{1,0:T(1,128)S(1)} %bitcast.1, ...), custom_call_target="tpu_custom_call" | custom-call | tf_op jit(solution)/shard_map/pallas_call | solution.py:352
  94.6 0.6 copy.14
  95.2 0.6 copy.15
Async XLA Ops:
  0.6 1.2 %copy-start = (bf16[8,512,128]{2,1,0:T(8,128)(2,1)S(1)}, bf16[8,512,128]{2,1,0:T(8,128)(2,1)}, u32[]{:S(2)}) copy-start(bf16[8,512,128]{2,1,0:T(8,128)(2,1)} %k_hbm.1) | copy-start | bytes 3145732
  1.9 1.2 %copy-start.1 = (bf16[8,512,128]{2,1,0:T(8,128)(2,1)S(1)}, bf16[8,512,128]{2,1,0:T(8,128)(2,1)}, u32[]{:S(2)}) copy-start(bf16[8,512,128]{2,1,0:T(8,128)(2,1)} %v_hbm.1) | copy-start | bytes 3145732
  3.1 0.8 copy-start.2
  3.8 0.7 copy-start.3
  4.5 0.7 copy-start.4
  5.2 0.7 copy-start.5
  5.9 0.7 copy-start.6

commit v2 on v0

v2 whole, which is shorter than its diff:
```python
import functools

import jax
import jax.numpy as jnp
from jax import lax
from jax.experimental import pallas as pl
from jax.experimental.pallas import tpu as pltpu
from jax.sharding import PartitionSpec as P

MESH = pl.DeviceIdType.MESH
F32, BF16 = jnp.float32, jnp.bfloat16
D = 8192
CHUNKS = 8
ROWS = 64
PART = 32
UNITS = 640
AT_ENDS = 1


def from_on(j, k):
    return (j + 8 - k) // 8


def chunk_of(j, x, zh):
    dx = from_on(j, 2) + from_on(j, 3) - from_on(j, 4) + from_on(j, 5) + from_on(j, 6)
    flip = from_on(j, 1) - from_on(j, 2) + from_on(j, 4) - from_on(j, 7)
    return dx, flip, ((x + dx) % 4) * 2 + (zh + flip) % 2


def kernel(
    q_hbm, nk_hbm, tv_hbm, len_hbm, gain_hbm, k_hbm, v_hbm, wg_hbm, wu_hbm, wd_hbm,
    attn_ref, out_ref,
    q_ref, nk_ref, tv_ref, len_ref, gain_ref, kbuf, vbuf, wgu, wd,
    qs, os, col, scales, sums, ssr, xblk, xall, xg, part, pout, pin, mout, min_, hbuf, cs, sr, cy, cr, acc, xcs, xcr, zcs, zcr,
    load_sem, ss_send, ss_recv, z_send, z_recv, y_send, y_recv, x_send, x_recv, f_send, f_recv,
    p_send, p_recv, m_send, m_recv, e_recv, h_send, h_recv, s_send, s_recv, c_send, c_recv, xc_send, xc_recv, zc_send, zc_recv,
):
    a = lax.axis_index("attn")
    zl = lax.axis_index("ffn")
    c = a % 2
    y = (a // 2) % 4
    zh = (a // 8) % 2
    x = a // 16
    slot = y * 2 + c

    def at(x_, zh_, slot_, zl_=None):
        return {"attn": (x_ * 2 + zh_) * 8 + slot_, "ffn": zl if zl_ is None else zl_}

    sibling = at(x, zh, y * 2 + (1 - c))
    partner = at(x, 1 - zh, slot)

    def remote(src, dst, send, recv, device):
        return pltpu.make_async_remote_copy(
            src_ref=src, dst_ref=dst, send_sem=send, recv_sem=recv, device_id=device, device_id_type=MESH
        )

    pairs = [
        (q_hbm, q_ref), (nk_hbm, nk_ref), (len_hbm, len_ref), (k_hbm, kbuf), (tv_hbm, tv_ref), (v_hbm, vbuf), (gain_hbm, gain_ref),
        (wg_hbm, wgu.at[:, pl.ds(0, UNITS)]), (wu_hbm, wgu.at[:, pl.ds(UNITS, UNITS)]), (wd_hbm, wd),
    ]
    loads = [pltpu.make_async_copy(src, dst, load_sem.at[n]) for n, (src, dst) in enumerate(pairs)]
    for load in loads[:7]:
        load.start()

    barrier = pltpu.get_barrier_semaphore()
    peers = [at(x, zh, (slot + d) % 8) for d in range(1, 8)]
    peers += [at((x + d) % 4, zh, slot) for d in range(1, 4)]
    peers += [at(x, zh, slot, (zl + d) % 4) for d in range(1, 4)]
    peers += [at((x + d) % 4, 1 - zh, slot) for d in range(4)]
    for peer in peers:
        pl.semaphore_signal(barrier, inc=1, device_id=peer, device_id_type=MESH)

    for load in loads[:7]:
        load.wait()
    for load in loads[7:]:
        load.start()
    qf = q_ref[...].astype(F32)
    for g in range(16):
        qs[pl.ds(g * 8, 8), :] = qf[:, g * 128 : (g + 1) * 128]
    nk = nk_ref[...].astype(F32)
    tv = tv_ref[...].astype(F32)
    scaling = 1.0 / 128**0.5
    position = lax.broadcasted_iota(jnp.int32, (16, 512), 1)
    for r in range(8):
        q = qs[pl.ds(r, 16, stride=8), :]
        scores = lax.dot_general(
            q.astype(BF16), kbuf[r], (((1,), (1,)), ((), ())), preferred_element_type=F32
        ) * scaling
        own = jnp.sum(q * nk[r : r + 1, :], axis=1, keepdims=True) * scaling
        live = position < len_ref[r]
        scores = jnp.where(live, scores, -1e30)
        largest = jnp.maximum(jnp.max(scores, axis=1, keepdims=True), own)
        weights = jnp.where(live, jnp.exp(scores - largest), 0.0)
        own_weight = jnp.exp(own - largest)
        total = jnp.sum(weights, axis=1, keepdims=True) + own_weight
        probs = (weights / total).astype(BF16)
        own_prob = (own_weight / total).astype(BF16).astype(F32)
        out = jnp.dot(probs, vbuf[r], preferred_element_type=F32)
        os[pl.ds(r, 16, stride=8), :] = out + own_prob * tv[r : r + 1, :]
    attn = jnp.concatenate([os[pl.ds(g * 8, 8), :] for g in range(16)], axis=1).astype(BF16)
    attn_ref[...] = attn
    feats = attn.astype(F32)
    xblk[0, slot] = jnp.concatenate([feats[:, :1024], feats[:, 1024:]], axis=0).astype(BF16)
    col[...] = jnp.zeros_like(col)

    pl.semaphore_wait(barrier, len(peers))

    z_copy = remote(xblk.at[0, slot], xblk.at[1, slot], z_send, z_recv, partner)
    z_copy.start()

    def y_copy(w, d):
        return remote(
            xblk.at[w, slot], xblk.at[w, slot], y_send, y_recv.at[w], at(x, zh, (slot + d) % 8)
        )

    def wait_send(ref, sem):
        remote(ref, ref, sem, sem, sibling).wait_send()

    def wait_recv(ref, sem):
        remote(ref, ref, sem, sem, sibling).wait_recv()

    def own_chunk(w):
        return x * 2 + (zh + w) % 2

    def x_copy(w, d):
        n = own_chunk(w)
        return remote(
            xall.at[n, c], xall.at[n, c], x_send, x_recv.at[n], at((x + d) % 4, zh, slot)
        )

    def assemble(w):
        n = own_chunk(w)
        wait_recv(xblk.at[w, pl.ds(0, 7)], y_recv.at[w])
        for b in range(4):
            first = xblk[w, 2 * b].astype(F32)
            second = xblk[w, 2 * b + 1].astype(F32)
            for h in range(2):
                pair = [first[8 * h : 8 * h + 8], second[8 * h : 8 * h + 8]]
                xall[n, h, pl.ds(16 * b, 16), :] = jnp.concatenate(pair, axis=0).astype(BF16)
        for d in range(1, 4):
            x_copy(w, d).start()

    for d in range(1, 8):
        y_copy(0, d).start()
    assemble(0)
    z_copy.wait_recv()
    for d in range(1, 8):
        y_copy(1, d).start()
    for load in loads[7:]:
        load.wait()

    side = zl // 2
    middle = zl * (3 - zl) // 2
    here = at(x, zh, slot, 1 + side)
    across = at(x, zh, slot, 2 - side)
    near_end = at(x, zh, slot, 3 * side)
    far_end = at(x, zh, slot, 3 - 3 * side)

    def p_copy(j, half, to):
        return remote(pout.at[2 * j + half], pin.at[2 * j + half], p_send, p_recv.at[j, half], to)

    def m_copy(j):
        return remote(mout.at[j], min_.at[j], m_send, m_recv.at[j], across)

    def ss_copy(j, to):
        return remote(ssr.at[4 * j + zl], ssr.at[4 * j + zl], ss_send, ss_recv.at[j], to)

    def h_copy(j, half, n, to):
        piece = hbuf.at[j, half]
        return remote(piece, piece, h_send.at[n], h_recv.at[j], to)

    def end_h_copy(j):
        piece = hbuf.at[j, 1 - side]
        return remote(piece, piece, h_send.at[0], e_recv.at[j], here)

    def activate(j):
        wait_recv(ssr.at[pl.ds(0, 3)], ss_recv.at[j])
        squares = ssr[4 * j] + ssr[4 * j + 1] + ssr[4 * j + 2] + ssr[4 * j + 3]
        scale = lax.rsqrt(squares[:1] / D + 1e-05)
        scales[...] = jnp.broadcast_to(scale, (128, 128)).T
        scale = scales[pl.ds(pl.multiple_of((1 - side) * PART, PART), PART), :][:, :1]
        wait_recv(pin.at[0], p_recv.at[j, 1 - side])
        sums[...] = part[j, 1 - side] + pin[2 * j + 1 - side].astype(F32)

        @pl.when(middle == 1)
        def _():
            wait_recv(min_.at[j], m_recv.at[j])
            sums[...] += min_[j].astype(F32)

        gate, up = sums[:, pl.ds(0, UNITS)] * scale, sums[:, pl.ds(UNITS, UNITS)] * scale
        hidden = gate / (1.0 + jnp.exp(-gate)) * up
        hbuf[j, 1 - side] = hidden.astype(BF16)

    def forward(j):
        n = chunk_of(j, x, zh)[2]
        return remote(xall.at[n, c], xall.at[n, c], f_send, f_recv.at[j], sibling)

    def s_copy(j):
        return remote(cs.at[j, 1 - c], sr.at[j], s_send, s_recv.at[j], sibling)

    def c_copy(j, d):
        to = (y + d) % 4
        return remote(cy.at[j, to], cr.at[j, y], c_send, c_recv.at[j], at(x, zh, to * 2 + c))

    def xc_copy(dx):
        return remote(xcs.at[dx - 1], xcr.at[dx - 1], xc_send, xc_recv, at((x + dx) % 4, zh, slot))

    def zc_copy(dx):
        return remote(zcs.at[dx], zcr.at[dx], zc_send, zc_recv, at((x + dx) % 4, 1 - zh, slot))

    def body(i, carry):
        @pl.when(i < CHUNKS)
        def _():
            n = chunk_of(i, x, zh)[2]

            @pl.when(i >= 2)
            def _():
                wait_recv(xall.at[n, 1 - c], f_recv.at[i])

            for b in range(4):
                rows = pl.ds(16 * b, 16)
                squares = 0.0
                for h in range(2):
                    feats = xall[n, h, rows, :].astype(F32)
                    xg[h, rows, :] = (feats * gain_ref[:, pl.ds(1024 * h, 1024)]).astype(BF16)
                    squares = squares + jnp.sum(feats * feats, axis=1, keepdims=True)
                col[rows, :] = jnp.broadcast_to(squares, (16, 128))
            ssr[4 * i + zl] = col[...].T[:8]

            @pl.when((middle == 0) & (i < AT_ENDS))
            def _():
                ss_copy(i, far_end).start()

            @pl.when((middle == 0) & (i >= AT_ENDS))
            def _():
                ss_copy(i, here).start()
                ss_copy(i, across).start()

            @pl.when((middle == 1) & (i < AT_ENDS))
            def _():
                ss_copy(i, near_end).start()
                ss_copy(i, far_end).start()

            @pl.when((middle == 1) & (i >= AT_ENDS))
            def _():
                ss_copy(i, across).start()

            for t in range(5):
                cols = pl.ds(t * 256, 256)
                tile = jnp.dot(xg[0], wgu[pl.ds(0, 1024), cols], preferred_element_type=F32) + jnp.dot(
                    xg[1], wgu[pl.ds(1024, 1024), cols], preferred_element_type=F32
                )
                for half in range(2):
                    part[i, half, :, cols] = tile[half * PART : (half + 1) * PART]

            @pl.when(middle == 0)
            def _():
                pout[2 * i + side] = part[i, side].astype(BF16)
                p_copy(i, side, here).start()

                @pl.when(i >= AT_ENDS)
                def _():
                    pout[2 * i + 1 - side] = part[i, 1 - side].astype(BF16)
                    p_copy(i, 1 - side, here).start()

        k = i - 6

        @pl.when((middle == 1) & (k >= 0) & (k < AT_ENDS))
        def _():
            wait_recv(hbuf.at[k, 1 - side], e_recv.at[k])
            h_copy(k, 1 - side, 0, across).start()

        k = i - 3

        @pl.when((middle == 1) & (k >= 0) & (k < AT_ENDS))
        def _():
            wait_recv(min_.at[k], m_recv.at[k])
            pout[2 * k + 1 - side] = (part[k, 1 - side] + min_[k].astype(F32)).astype(BF16)
            p_copy(k, 1 - side, near_end).start()

        @pl.when((middle == 1) & (k >= AT_ENDS) & (k < CHUNKS))
        def _():
            activate(k)
            h_copy(k, 1 - side, 0, across).start()
            h_copy(k, 1 - side, 2, far_end).start()
            h_copy(k, 1 - side, 1, near_end).start()

        u = i - 1

        @pl.when((middle == 1) & (u >= 0) & (u < CHUNKS))
        def _():
            wait_recv(pin.at[0], p_recv.at[u, side])
            mout[u] = (part[u, side] + pin[2 * u + side].astype(F32)).astype(BF16)
            m_copy(u).start()

        k = i - 4

        @pl.when((middle == 0) & (k >= 0) & (k < AT_ENDS))
        def _():
            activate(k)
            end_h_copy(k).start()

        def down(late, carry):
            j = i - 8 + middle + 2 * late

            @pl.when((j >= AT_ENDS * late) & (j < AT_ENDS + (CHUNKS - AT_ENDS) * late))
            def _():
                @pl.when((middle == 0) & (j >= AT_ENDS))
                def _():
                    wait_recv(hbuf.at[j], h_recv.at[j])

                @pl.when((middle == 1) | (j < AT_ENDS))
                def _():
                    wait_recv(hbuf.at[j, side], h_recv.at[j])

                @pl.when((middle == 1) & (j < AT_ENDS))
                def _():
                    h_copy(j, side, 1, near_end).start()

                hidden = jnp.concatenate([hbuf[j, 0], hbuf[j, 1]], axis=0)
                for t in range(4):
                    left = jnp.dot(hidden, wd[:, pl.ds(t * 256, 256)], preferred_element_type=F32)
                    right = jnp.dot(hidden, wd[:, pl.ds(1024 + t * 256, 256)], preferred_element_type=F32)
                    for b in range(8):
                        block = jnp.concatenate([left[b * 8 : b * 8 + 8], right[b * 8 : b * 8 + 8]], axis=0)
                        cs[j, b % 2, b // 2, :, pl.ds(t * 256, 256)] = block.astype(BF16)
                s_copy(j).start()

            return carry

        lax.fori_loop(0, 2, down, 0)

        def pair(late, carry):
            j = i - 9 + middle + 2 * late

            @pl.when((j >= AT_ENDS * late) & (j < AT_ENDS + (CHUNKS - AT_ENDS) * late))
            def _():
                wait_recv(sr.at[j], s_recv.at[j])
                for b in range(4):
                    cy[j, b] = (cs[j, c, b].astype(F32) + sr[j, b].astype(F32)).astype(BF16)
                for d in range(1, 4):
                    c_copy(j, d).start()
                cr[j, y] = cy[j, y]

            return carry

        lax.fori_loop(0, 2, pair, 0)

        m = i - 11 + middle

        @pl.when((m >= 0) & (m < CHUNKS))
        def _():
            wait_recv(cr.at[m, pl.ds(0, 3)], c_recv.at[m])
            total = cr[m, 0].astype(F32)
            for b in range(1, 4):
                total = total + cr[m, b].astype(F32)
            dx, flip, _ = chunk_of(m, x, zh)

            @pl.when(m == 0)
            def _():
                acc[...] = total

            @pl.when((m > 0) & (flip == 0))
            def _():
                xcs[dx - 1] = total.astype(BF16)
                xc_copy(dx).start()

            @pl.when(flip == 1)
            def _():
                zcs[dx] = total.astype(BF16)
                zc_copy(dx).start()

        @pl.when(i == 0)
        def _():
            assemble(1)

        for when, ready in ((1, (2, 3)), (2, (7,)), (3, (4, 5)), (4, (6,))):

            @pl.when(i == when)
            def _():
                for j in ready:
                    n = chunk_of(j, x, zh)[2]
                    wait_recv(xall.at[n, c], x_recv.at[n])
                    forward(j).start()

        return carry

    lax.fori_loop(0, CHUNKS + 11, body, 0)

    wait_recv(zcr, zc_recv)
    total = acc[...]
    for dx in range(4):
        total = total + zcr[dx].astype(F32)
    wait_recv(xcr, xc_recv)
    for dx in range(3):
        total = total + xcr[dx].astype(F32)
    out_ref[...] = jnp.concatenate([total[:8], total[8:]], axis=1).astype(BF16)

    z_copy.wait_send()
    wait_send(xblk.at[:, pl.ds(0, 7)], y_send)
    wait_send(xall.at[pl.ds(0, 6), 0], x_send)
    wait_send(xall.at[pl.ds(0, 6), 0], f_send)
    wait_send(cs.at[:, 0], s_send)
    wait_send(cy.at[:, pl.ds(0, 3)], c_send)
    wait_send(xcs, xc_send)
    wait_send(zcs, zc_send)

    @pl.when(middle == 0)
    def _():
        wait_send(pout.at[pl.ds(0, 2 * CHUNKS - AT_ENDS)], p_send)
        wait_send(ssr.at[pl.ds(0, 2 * CHUNKS - AT_ENDS)], ss_send)
        wait_send(hbuf.at[pl.ds(0, AT_ENDS), 0], h_send.at[0])

    @pl.when(middle == 1)
    def _():
        wait_send(pout.at[pl.ds(0, AT_ENDS)], p_send)
        wait_send(ssr.at[pl.ds(0, CHUNKS + AT_ENDS)], ss_send)
        wait_send(mout, m_send)
        wait_send(hbuf.at[:, 0], h_send.at[0])
        wait_send(hbuf.at[:, 0], h_send.at[1])
        wait_send(hbuf.at[pl.ds(0, CHUNKS - AT_ENDS), 0], h_send.at[2])


def local(queries, cache_keys, value_cache, new_keys, token_values, lengths, norm_gain, w_gate, w_up, w_down):
    vmem = pl.BlockSpec(memory_space=pltpu.VMEM)
    hbm = pl.BlockSpec(memory_space=pltpu.HBM)
    dma = pltpu.SemaphoreType.DMA
    return pl.pallas_call(
        kernel,
        out_shape=(jax.ShapeDtypeStruct((8, 2048), BF16), jax.ShapeDtypeStruct((8, 2048), BF16)),
        in_specs=[hbm] * 10,
        out_specs=(vmem, vmem),
        scratch_shapes=[
            pltpu.VMEM((8, 2048), BF16),
            pltpu.VMEM((8, 128), BF16),
            pltpu.VMEM((8, 128), BF16),
            pltpu.SMEM((8,), jnp.int32),
            pltpu.VMEM((1, 2048), F32),
            pltpu.VMEM((8, 512, 128), BF16),
            pltpu.VMEM((8, 512, 128), BF16),
            pltpu.VMEM((2048, 2 * UNITS), BF16),
            pltpu.VMEM((UNITS, 2048), BF16),
            pltpu.VMEM((128, 128), F32),
            pltpu.VMEM((128, 128), F32),
            pltpu.VMEM((128, 128), F32),
            pltpu.VMEM((128, 128), F32),
            pltpu.VMEM((PART, 2 * UNITS), F32),
            pltpu.VMEM((4 * CHUNKS, 8, 128), F32),
            pltpu.VMEM((2, 8, 16, 1024), BF16),
            pltpu.VMEM((CHUNKS, 2, ROWS, 1024), BF16),
            pltpu.VMEM((2, ROWS, 1024), BF16),
            pltpu.VMEM((CHUNKS, 2, PART, 2 * UNITS), F32),
            pltpu.VMEM((2 * CHUNKS, PART, 2 * UNITS), BF16),
            pltpu.VMEM((2 * CHUNKS, PART, 2 * UNITS), BF16),
            pltpu.VMEM((CHUNKS, PART, 2 * UNITS), BF16),
            pltpu.VMEM((CHUNKS, PART, 2 * UNITS), BF16),
            pltpu.VMEM((CHUNKS, 2, PART, UNITS), BF16),
            pltpu.VMEM((CHUNKS, 2, 4, 16, 1024), BF16),
            pltpu.VMEM((CHUNKS, 4, 16, 1024), BF16),
            pltpu.VMEM((CHUNKS, 4, 16, 1024), BF16),
            pltpu.VMEM((CHUNKS, 4, 16, 1024), BF16),
            pltpu.VMEM((16, 1024), F32),
            pltpu.VMEM((3, 16, 1024), BF16),
            pltpu.VMEM((3, 16, 1024), BF16),
            pltpu.VMEM((4, 16, 1024), BF16),
            pltpu.VMEM((4, 16, 1024), BF16),
            dma((10,)),
            dma, dma((CHUNKS,)),
            dma, dma,
            dma, dma((2,)),
            dma, dma((CHUNKS,)),
            dma, dma((CHUNKS,)),
            dma, dma((CHUNKS, 2)),
            dma, dma((CHUNKS,)),
            dma((CHUNKS,)),
            dma((3,)), dma((CHUNKS,)),
            dma, dma((CHUNKS,)),
            dma, dma((CHUNKS,)),
            dma, dma,
            dma, dma,
        ],
        compiler_params=pltpu.CompilerParams(
            collective_id=0, has_side_effects=True, vmem_limit_bytes=60 * 1024 * 1024
        ),
    )(queries, new_keys, token_values, lengths, norm_gain.reshape(1, 2048), cache_keys, value_cache, w_gate, w_up, w_down)


def solution(mesh):
    in_specs = (
        P("attn", "ffn"),
        P("attn", None, "ffn"),
        P("attn", None, "ffn"),
        P("attn", "ffn"),
        P("attn", "ffn"),
        P("attn"),
        P("ffn"),
        P("ffn", "attn"),
        P("ffn", "attn"),
        P("attn", "ffn"),
    )
    out_specs = (P("attn", "ffn"), P("attn", "ffn"))
    return jax.shard_map(local, mesh=mesh, in_specs=in_specs, out_specs=out_specs, check_vma=False)
```

time: 658 us -> 74.6 us (0.11)
  the two profiles are of different devices: /device:TPU:32 before, /device:TPU:2 now
where the time goes in v2:
time: 74.6 us; the launch traced here: 74.3 us
  Pallas kernels  71 us (95%)
  local copies, waits for them, and re-layouts  2.75 us (4%)
    pallas_call x1, Pallas kernels, local(): pl.pallas_call(kernel, out_shape=(jax.ShapeDtypeStruct((8, 2048), BF16),...  71 us
    unnamed x2, local copies, waits for them, and re-layouts  2.75 us

profile of v2, /device:TPU:2, one launch (start us, length us, event | category | flops | bytes accessed | tf_op | source)
XLA Modules:
  0.0 74.3 jit_solution(6835777858352154245)
XLA Ops:
  0.6 71.0 %shard_map.113 = (bf16[8,2048]{1,0:T(8,128)(2,1)}, bf16[8,2048]{1,0:T(8,128)(2,1)}) custom-call(bf16[8,2048]{1,0:T(8,128)(2,1)} %q_hbm.1, bf16[8,128]{1,0:T(8,128)(2,1)} %nk_hbm.1, bf16[8,128]{1,0:T(8,128)(2,1)} %tv_hbm.1, s32[8]{0:T(128)} %len_hbm.1, f32[1,2048]{1,0:T(1,128)} %bitcast.1, bf16[8,512,128]{2,1,0:T(8,128)(2,1)} %k_hbm.1, ...), custom_call_target="tpu_custom_call" | custom-call | tf_op jit(solution)/shard_map/pallas_call | solution.py:428
  71.6 1.4 %copy.14 = bf16[8,2048]{1,0:T(8,128)(2,1)} copy(bf16[8,2048]{1,0:T(8,128)(2,1)} %get-tuple-element.4) | data formatting | bytes 65536
  73.0 1.4 %copy.15 = bf16[8,2048]{1,0:T(8,128)(2,1)} copy(bf16[8,2048]{1,0:T(8,128)(2,1)} %get-tuple-element.5) | data formatting | bytes 65536

commit v3 on v2

--- a/solution.py
+++ b/solution.py
@@ -14,7 +14,8 @@
 ROWS = 64
 PART = 32
 UNITS = 640
-AT_ENDS = 1
+FORWARDED = 6
+END_LAG = 7
 
 
 def from_on(j, k):
@@ -29,11 +30,11 @@
 
 def kernel(
     q_hbm, nk_hbm, tv_hbm, len_hbm, gain_hbm, k_hbm, v_hbm, wg_hbm, wu_hbm, wd_hbm,
-    attn_ref, out_ref,
+    out_ref,
     q_ref, nk_ref, tv_ref, len_ref, gain_ref, kbuf, vbuf, wgu, wd,
     qs, os, col, scales, sums, ssr, xblk, xall, xg, part, pout, pin, mout, min_, hbuf, cs, sr, cy, cr, acc, xcs, xcr, zcs, zcr,
     load_sem, ss_send, ss_recv, z_send, z_recv, y_send, y_recv, x_send, x_recv, f_send, f_recv,
-    p_send, p_recv, m_send, m_recv, e_recv, h_send, h_recv, s_send, s_recv, c_send, c_recv, xc_send, xc_recv, zc_send, zc_recv,
+    p_send, p_recv, m_send, m_recv, h_send, h_recv, s_send, s_recv, c_send, c_recv, xc_send, xc_recv, zc_send, zc_recv,
 ):
     a = lax.axis_index("attn")
     zl = lax.axis_index("ffn")
@@ -98,7 +99,7 @@
         out = jnp.dot(probs, vbuf[r], preferred_element_type=F32)
         os[pl.ds(r, 16, stride=8), :] = out + own_prob * tv[r : r + 1, :]
     attn = jnp.concatenate([os[pl.ds(g * 8, 8), :] for g in range(16)], axis=1).astype(BF16)
-    attn_ref[...] = attn
+    out_ref[pl.ds(0, 8), :] = attn.astype(F32)
     feats = attn.astype(F32)
     xblk[0, slot] = jnp.concatenate([feats[:, :1024], feats[:, 1024:]], axis=0).astype(BF16)
     col[...] = jnp.zeros_like(col)
@@ -169,24 +170,15 @@
         piece = hbuf.at[j, half]
         return remote(piece, piece, h_send.at[n], h_recv.at[j], to)
 
-    def end_h_copy(j):
-        piece = hbuf.at[j, 1 - side]
-        return remote(piece, piece, h_send.at[0], e_recv.at[j], here)
-
     def activate(j):
         wait_recv(ssr.at[pl.ds(0, 3)], ss_recv.at[j])
         squares = ssr[4 * j] + ssr[4 * j + 1] + ssr[4 * j + 2] + ssr[4 * j + 3]
-        scale = lax.rsqrt(squares[:1] / D + 1e-05)
+        scale = lax.rsqrt(squares / D + 1e-05)
         scales[...] = jnp.broadcast_to(scale, (128, 128)).T
         scale = scales[pl.ds(pl.multiple_of((1 - side) * PART, PART), PART), :][:, :1]
         wait_recv(pin.at[0], p_recv.at[j, 1 - side])
-        sums[...] = part[j, 1 - side] + pin[2 * j + 1 - side].astype(F32)
-
-        @pl.when(middle == 1)
-        def _():
-            wait_recv(min_.at[j], m_recv.at[j])
-            sums[...] += min_[j].astype(F32)
-
+        wait_recv(min_.at[j], m_recv.at[j])
+        sums[...] = part[j, 1 - side] + pin[2 * j + 1 - side].astype(F32) + min_[j].astype(F32)
         gate, up = sums[:, pl.ds(0, UNITS)] * scale, sums[:, pl.ds(UNITS, UNITS)] * scale
         hidden = gate / (1.0 + jnp.exp(-gate)) * up
         hbuf[j, 1 - side] = hidden.astype(BF16)
@@ -209,6 +201,8 @@
         return remote(zcs.at[dx], zcr.at[dx], zc_send, zc_recv, at((x + dx) % 4, 1 - zh, slot))
 
     def body(i, carry):
+        lag = 4 + (END_LAG - 4) * (1 - middle)
+
         @pl.when(i < CHUNKS)
         def _():
             n = chunk_of(i, x, zh)[2]
@@ -225,23 +219,14 @@
                     xg[h, rows, :] = (feats * gain_ref[:, pl.ds(1024 * h, 1024)]).astype(BF16)
                     squares = squares + jnp.sum(feats * feats, axis=1, keepdims=True)
                 col[rows, :] = jnp.broadcast_to(squares, (16, 128))
-            ssr[4 * i + zl] = col[...].T[:8]
-
-            @pl.when((middle == 0) & (i < AT_ENDS))
-            def _():
-                ss_copy(i, far_end).start()
-
-            @pl.when((middle == 0) & (i >= AT_ENDS))
+            ssr[4 * i + zl] = col[...].T[:1]
+
+            @pl.when(middle == 0)
             def _():
                 ss_copy(i, here).start()
                 ss_copy(i, across).start()
 
-            @pl.when((middle == 1) & (i < AT_ENDS))
-            def _():
-                ss_copy(i, near_end).start()
-                ss_copy(i, far_end).start()
-
-            @pl.when((middle == 1) & (i >= AT_ENDS))
+            @pl.when(middle == 1)
             def _():
                 ss_copy(i, across).start()
 
@@ -255,35 +240,32 @@
 
             @pl.when(middle == 0)
             def _():
-                pout[2 * i + side] = part[i, side].astype(BF16)
-                p_copy(i, side, here).start()
-
-                @pl.when(i >= AT_ENDS)
-                def _():
-                    pout[2 * i + 1 - side] = part[i, 1 - side].astype(BF16)
-                    p_copy(i, 1 - side, here).start()
-
-        k = i - 6
-
-        @pl.when((middle == 1) & (k >= 0) & (k < AT_ENDS))
-        def _():
-            wait_recv(hbuf.at[k, 1 - side], e_recv.at[k])
-            h_copy(k, 1 - side, 0, across).start()
+                for half in (side, 1 - side):
+                    pout[2 * i + half] = part[i, half].astype(BF16)
+                    p_copy(i, half, here).start()
+
+        g = i - lag - 1
+
+        @pl.when((g >= 0) & (g < CHUNKS))
+        def _():
+            wait_recv(sr.at[g], s_recv.at[g])
+            for b in range(4):
+                cy[g, b] = (cs[g, c, b].astype(F32) + sr[g, b].astype(F32)).astype(BF16)
+            for d in range(1, 4):
+                c_copy(g, d).start()
+            cr[g, y] = cy[g, y]
 
         k = i - 3
 
-        @pl.when((middle == 1) & (k >= 0) & (k < AT_ENDS))
-        def _():
-            wait_recv(min_.at[k], m_recv.at[k])
-            pout[2 * k + 1 - side] = (part[k, 1 - side] + min_[k].astype(F32)).astype(BF16)
-            p_copy(k, 1 - side, near_end).start()
-
-        @pl.when((middle == 1) & (k >= AT_ENDS) & (k < CHUNKS))
+        @pl.when((middle == 1) & (k >= 0) & (k < CHUNKS))
         def _():
             activate(k)
             h_copy(k, 1 - side, 0, across).start()
-            h_copy(k, 1 - side, 2, far_end).start()
             h_copy(k, 1 - side, 1, near_end).start()
+
+            @pl.when(k >= FORWARDED)
+            def _():
+                h_copy(k, 1 - side, 2, far_end).start()
 
         u = i - 1
 
@@ -293,60 +275,32 @@
             mout[u] = (part[u, side] + pin[2 * u + side].astype(F32)).astype(BF16)
             m_copy(u).start()
 
-        k = i - 4
-
-        @pl.when((middle == 0) & (k >= 0) & (k < AT_ENDS))
-        def _():
-            activate(k)
-            end_h_copy(k).start()
-
-        def down(late, carry):
-            j = i - 8 + middle + 2 * late
-
-            @pl.when((j >= AT_ENDS * late) & (j < AT_ENDS + (CHUNKS - AT_ENDS) * late))
-            def _():
-                @pl.when((middle == 0) & (j >= AT_ENDS))
+        j = i - lag
+
+        @pl.when((j >= 0) & (j < CHUNKS))
+        def _():
+            @pl.when(middle == 0)
+            def _():
+                wait_recv(hbuf.at[j], h_recv.at[j])
+
+            @pl.when(middle == 1)
+            def _():
+                wait_recv(hbuf.at[j, side], h_recv.at[j])
+
+                @pl.when(j < FORWARDED)
                 def _():
-                    wait_recv(hbuf.at[j], h_recv.at[j])
-
-                @pl.when((middle == 1) | (j < AT_ENDS))
-                def _():
-                    wait_recv(hbuf.at[j, side], h_recv.at[j])
-
-                @pl.when((middle == 1) & (j < AT_ENDS))
-                def _():
-                    h_copy(j, side, 1, near_end).start()
-
-                hidden = jnp.concatenate([hbuf[j, 0], hbuf[j, 1]], axis=0)
-                for t in range(4):
-                    left = jnp.dot(hidden, wd[:, pl.ds(t * 256, 256)], preferred_element_type=F32)
-                    right = jnp.dot(hidden, wd[:, pl.ds(1024 + t * 256, 256)], preferred_element_type=F32)
-                    for b in range(8):
-                        block = jnp.concatenate([left[b * 8 : b * 8 + 8], right[b * 8 : b * 8 + 8]], axis=0)
-                        cs[j, b % 2, b // 2, :, pl.ds(t * 256, 256)] = block.astype(BF16)
-                s_copy(j).start()
-
-            return carry
-
-        lax.fori_loop(0, 2, down, 0)
-
-        def pair(late, carry):
-            j = i - 9 + middle + 2 * late
-
-            @pl.when((j >= AT_ENDS * late) & (j < AT_ENDS + (CHUNKS - AT_ENDS) * late))
-            def _():
-                wait_recv(sr.at[j], s_recv.at[j])
-                for b in range(4):
-                    cy[j, b] = (cs[j, c, b].astype(F32) + sr[j, b].astype(F32)).astype(BF16)
-                for d in range(1, 4):
-                    c_copy(j, d).start()
-                cr[j, y] = cy[j, y]
-
-            return carry
-
-        lax.fori_loop(0, 2, pair, 0)
-
-        m = i - 11 + middle
+                    h_copy(j, side, 2, near_end).start()
+
+            hidden = jnp.concatenate([hbuf[j, 0], hbuf[j, 1]], axis=0)
+            for t in range(4):
+                left = jnp.dot(hidden, wd[:, pl.ds(t * 256, 256)], preferred_element_type=F32)
+                right = jnp.dot(hidden, wd[:, pl.ds(1024 + t * 256, 256)], preferred_element_type=F32)
+                for b in range(8):
+                    block = jnp.concatenate([left[b * 8 : b * 8 + 8], right[b * 8 : b * 8 + 8]], axis=0)
+                    cs[j, b % 2, b // 2, :, pl.ds(t * 256, 256)] = block.astype(BF16)
+            s_copy(j).start()
+
+        m = i - lag - 2
 
         @pl.when((m >= 0) & (m < CHUNKS))
         def _():
@@ -385,7 +339,7 @@
 
         return carry
 
-    lax.fori_loop(0, CHUNKS + 11, body, 0)
+    lax.fori_loop(0, CHUNKS + END_LAG + 2, body, 0)
 
     wait_recv(zcr, zc_recv)
     total = acc[...]
@@ -394,7 +348,7 @@
     wait_recv(xcr, xc_recv)
     for dx in range(3):
         total = total + xcr[dx].astype(F32)
-    out_ref[...] = jnp.concatenate([total[:8], total[8:]], axis=1).astype(BF16)
+    out_ref[pl.ds(8, 8), :] = jnp.concatenate([total[:8], total[8:]], axis=1)
 
     z_copy.wait_send()
     wait_send(xblk.at[:, pl.ds(0, 7)], y_send)
@@ -407,29 +361,26 @@
 
     @pl.when(middle == 0)
     def _():
-        wait_send(pout.at[pl.ds(0, 2 * CHUNKS - AT_ENDS)], p_send)
-        wait_send(ssr.at[pl.ds(0, 2 * CHUNKS - AT_ENDS)], ss_send)
-        wait_send(hbuf.at[pl.ds(0, AT_ENDS), 0], h_send.at[0])
+        wait_send(pout, p_send)
+        wait_send(ssr.at[pl.ds(0, 2 * CHUNKS)], ss_send)
 
     @pl.when(middle == 1)
     def _():
-        wait_send(pout.at[pl.ds(0, AT_ENDS)], p_send)
-        wait_send(ssr.at[pl.ds(0, CHUNKS + AT_ENDS)], ss_send)
+        wait_send(ssr.at[pl.ds(0, CHUNKS)], ss_send)
         wait_send(mout, m_send)
-        wait_send(hbuf.at[:, 0], h_send.at[0])
-        wait_send(hbuf.at[:, 0], h_send.at[1])
-        wait_send(hbuf.at[pl.ds(0, CHUNKS - AT_ENDS), 0], h_send.at[2])
+        for n in range(3):
+            wait_send(hbuf.at[:, 0], h_send.at[n])
 
 
 def local(queries, cache_keys, value_cache, new_keys, token_values, lengths, norm_gain, w_gate, w_up, w_down):
     vmem = pl.BlockSpec(memory_space=pltpu.VMEM)
     hbm = pl.BlockSpec(memory_space=pltpu.HBM)
     dma = pltpu.SemaphoreType.DMA
-    return pl.pallas_call(
+    both = pl.pallas_call(
         kernel,
-        out_shape=(jax.ShapeDtypeStruct((8, 2048), BF16), jax.ShapeDtypeStruct((8, 2048), BF16)),
+        out_shape=jax.ShapeDtypeStruct((16, 2048), F32),
         in_specs=[hbm] * 10,
-        out_specs=(vmem, vmem),
+        out_specs=vmem,
         scratch_shapes=[
             pltpu.VMEM((8, 2048), BF16),
             pltpu.VMEM((8, 128), BF16),
@@ -445,7 +396,7 @@
             pltpu.VMEM((128, 128), F32),
             pltpu.VMEM((128, 128), F32),
             pltpu.VMEM((PART, 2 * UNITS), F32),
-            pltpu.VMEM((4 * CHUNKS, 8, 128), F32),
+            pltpu.VMEM((4 * CHUNKS, 1, 128), F32),
             pltpu.VMEM((2, 8, 16, 1024), BF16),
             pltpu.VMEM((CHUNKS, 2, ROWS, 1024), BF16),
             pltpu.VMEM((2, ROWS, 1024), BF16),
@@ -472,7 +423,6 @@
             dma, dma((CHUNKS,)),
             dma, dma((CHUNKS, 2)),
             dma, dma((CHUNKS,)),
-            dma((CHUNKS,)),
             dma((3,)), dma((CHUNKS,)),
             dma, dma((CHUNKS,)),
             dma, dma((CHUNKS,)),
@@ -483,6 +433,7 @@
             collective_id=0, has_side_effects=True, vmem_limit_bytes=60 * 1024 * 1024
         ),
     )(queries, new_keys, token_values, lengths, norm_gain.reshape(1, 2048), cache_keys, value_cache, w_gate, w_up, w_down)
+    return both[:8].astype(BF16), both[8:].astype(BF16)
 
 
 def solution(mesh):

time: 74.6 us -> 71 us (0.952)
  Pallas kernels: 71 us -> 68.7 us
  local copies, waits for them, and re-layouts: 2.75 us -> 0.63 us
  other arithmetic: 0 us -> 0.91 us
    unnamed x2 -> x0, local copies, waits for them, and re-layouts: 2.75 us -> none
    pallas_call x1, Pallas kernels: 71 us -> 68.7 us  [local(): pl.pallas_call(kernel, out_shape=jax.ShapeDtypeStruct((16, 2048), F32), i...]
    another operation x0 -> x1, other arithmetic: none -> 0.91 us
where the time goes in v3:
time: 71 us; the launch traced here: 70.9 us
  Pallas kernels  68.7 us (97%)
  other arithmetic  0.91 us (1%)
    pallas_call x1, Pallas kernels, local(): pl.pallas_call(kernel, out_shape=jax.ShapeDtypeStruct((16, 2048), F32), i...  68.7 us

profile of v3, /device:TPU:2, one launch (start us, length us, event | category | flops | bytes accessed | tf_op | source)
XLA Modules:
  0.0 70.9 jit_solution(888915703275390434)
XLA Ops:
  0.6 68.7 %shard_map.113 = f32[16,2048]{1,0:T(8,128)} custom-call(bf16[8,2048]{1,0:T(8,128)(2,1)} %q_hbm.1, bf16[8,128]{1,0:T(8,128)(2,1)} %nk_hbm.1, bf16[8,128]{1,0:T(8,128)(2,1)} %tv_hbm.1, s32[8]{0:T(128)} %len_hbm.1, f32[1,2048]{1,0:T(1,128)} %bitcast.1, bf16[8,512,128]{2,1,0:T(8,128)(2,1)} %k_hbm.1, bf16[8,512,128]{2,1,0:T(8,128)(2,1)} %v_hbm.1, ...), custom_call_target="tpu_custom_call" | custom-call | tf_op jit(solution)/shard_map/pallas_call | solution.py:379
  69.4 0.9 %convert.4 = bf16[16,2048]{1,0:T(8,128)(2,1)S(1)} convert(f32[16,2048]{1,0:T(8,128)} %shard_map.113) | non-fusion elementwise | flops 32768 | bytes 196608 | tf_op jit(solution)/shard_map/convert.1
  70.3 0.6 fusion

commit v4 on v3

--- a/solution.py
+++ b/solution.py
@@ -267,14 +267,6 @@
             def _():
                 h_copy(k, 1 - side, 2, far_end).start()
 
-        u = i - 1
-
-        @pl.when((middle == 1) & (u >= 0) & (u < CHUNKS))
-        def _():
-            wait_recv(pin.at[0], p_recv.at[u, side])
-            mout[u] = (part[u, side] + pin[2 * u + side].astype(F32)).astype(BF16)
-            m_copy(u).start()
-
         j = i - lag
 
         @pl.when((j >= 0) & (j < CHUNKS))
@@ -299,6 +291,14 @@
                     block = jnp.concatenate([left[b * 8 : b * 8 + 8], right[b * 8 : b * 8 + 8]], axis=0)
                     cs[j, b % 2, b // 2, :, pl.ds(t * 256, 256)] = block.astype(BF16)
             s_copy(j).start()
+
+        u = i - 1
+
+        @pl.when((middle == 1) & (u >= 0) & (u < CHUNKS))
+        def _():
+            wait_recv(pin.at[0], p_recv.at[u, side])
+            mout[u] = (part[u, side] + pin[2 * u + side].astype(F32)).astype(BF16)
+            m_copy(u).start()
 
         m = i - lag - 2
 

time: 71 us -> 70.5 us (level)
  Pallas kernels: 68.7 us -> 67.7 us
    pallas_call x1, Pallas kernels: 68.7 us -> 67.7 us  [local(): pl.pallas_call(kernel, out_shape=jax.ShapeDtypeStruct((16, 2048), F32), i...]
where the time goes in v4:
time: 70.5 us; the launch traced here: 69.9 us
  Pallas kernels  67.7 us (96%)
  other arithmetic  0.91 us (1%)
    pallas_call x1, Pallas kernels, local(): pl.pallas_call(kernel, out_shape=jax.ShapeDtypeStruct((16, 2048), F32), i...  67.7 us

profile of v4, /device:TPU:2, one launch (start us, length us, event | category | flops | bytes accessed | tf_op | source)
XLA Modules:
  0.0 69.9 jit_solution(5459685698497315762)
XLA Ops:
  0.6 67.7 %shard_map.113 = f32[16,2048]{1,0:T(8,128)} custom-call(bf16[8,2048]{1,0:T(8,128)(2,1)} %q_hbm.1, bf16[8,128]{1,0:T(8,128)(2,1)} %nk_hbm.1, bf16[8,128]{1,0:T(8,128)(2,1)} %tv_hbm.1, s32[8]{0:T(128)} %len_hbm.1, f32[1,2048]{1,0:T(1,128)} %bitcast.1, bf16[8,512,128]{2,1,0:T(8,128)(2,1)} %k_hbm.1, bf16[8,512,128]{2,1,0:T(8,128)(2,1)} %v_hbm.1, ...), custom_call_target="tpu_custom_call" | custom-call | tf_op jit(solution)/shard_map/pallas_call | solution.py:379
  68.4 0.9 %convert.4 = bf16[16,2048]{1,0:T(8,128)(2,1)S(1)} convert(f32[16,2048]{1,0:T(8,128)} %shard_map.113) | non-fusion elementwise | flops 32768 | bytes 196608 | tf_op jit(solution)/shard_map/convert.1
  69.3 0.6 fusion
